TPU v7x, 32 devices: a whole 2x2x4 slice. The times are simulated.
32 devices in a mesh: expert: 16 (over z, y, x), replica: 2 (over core).
Axes of the slice: x: 2, y: 2, z: 4, core: 2. Of those that a mesh axis runs over, the one named last changes fastest.
Arguments:
- x_quant: bfloat16 [4096, 2048], P(('expert', 'replica')), may hold values from -6 to 6
- x_scale: float32 [4096, 16], P(('expert', 'replica')), may hold values from 0.3 to 3
- out_grad: bfloat16 [4096, 2048], P(('expert', 'replica')), may hold values from -6 to 6
- expert_ids: int32 [4096, 8], P(('expert', 'replica')), may hold values from 0 to 15, all different within a row; in each aligned block of 128 rows (0 to 127, 128 to 255, ...) at most 80 rows name the same one
- gate_fixed: int32 [4096, 8], P(('expert', 'replica')), may hold values from 1024 to 16383
- w_gate: bfloat16 [16, 2048, 768], P('expert'), may hold values from -0.125 to 0.125
- s_gate: float32 [16, 16, 6], P('expert'), may hold values from 0.3 to 3
- w_up: bfloat16 [16, 2048, 768], P('expert'), may hold values from -0.125 to 0.125
- s_up: float32 [16, 16, 6], P('expert'), may hold values from 0.3 to 3
- w_down: bfloat16 [16, 768, 2048], P('expert'), may hold values from -0.21875 to 0.21875
- s_down: float32 [16, 6, 16], P('expert'), may hold values from 0.3 to 3
Outputs:
- grad_input: bfloat16 [4096, 2048], P(('expert', 'replica'))
- grad_gate: bfloat16 [16, 2048, 768], P('expert', None, 'replica')
- grad_up: bfloat16 [16, 2048, 768], P('expert', None, 'replica')
- grad_down: bfloat16 [16, 768, 2048], P('expert', 'replica')
Inputs may be any that keep to these rules, and one draw needn't show every extreme that they name: `expert_ids`: each row names 8 different experts. Among the rows of one device at most 80 name the same expert, and in every draw some expert is named by exactly 80 rows of some device.
All inputs are finite; a program needn't handle non-finite values.
Results may differ from a plain program's by a relative error of at most 0.012.
Values may be sent and summed in bfloat16 or wider, within the bound.
A program may use at most 192 MiB of HBM per device.

v0:
```python
import jax
import jax.numpy as jnp
from jax import lax
from jax.experimental import pallas as pl
from jax.experimental.pallas import tpu as pltpu
from jax.sharding import PartitionSpec as P

DEPTH = 4


def place():
    me = lax.axis_index("expert")
    z, q = me // 4, me % 4
    x, y = q % 2, q // 2
    return me, z, q, q + 1 - 2 * x, q + 2 - 4 * y, 3 - q


def greet(me, z, qx, qy):
    barrier = pltpu.get_barrier_semaphore()
    for dev in (4 * z + qx, 4 * z + qy):
        pl.semaphore_signal(barrier, inc=1, device_id={"expert": dev})

    @pl.when(z > 0)
    def _():
        pl.semaphore_signal(barrier, inc=1, device_id={"expert": me - 4})

    @pl.when(z < DEPTH - 1)
    def _():
        pl.semaphore_signal(barrier, inc=1, device_id={"expert": me + 4})

    peers = 2 + jnp.minimum(z, 1) + jnp.minimum(DEPTH - 1 - z, 1)
    pl.semaphore_wait(barrier, peers)


def near_first(zz):
    return sorted(range(DEPTH), key=lambda s: (abs(s - zz), s))


def nt(a, b):
    return lax.dot_general(a, b, (((1,), (1,)), ((), ())), preferred_element_type=jnp.float32)


def rows_kernel(
    x_ref, g_ref, pick, pick_t, gates, gate_w, up_w, down_w,
    part, xrows, row_grad, hidden, gate_grad, up_grad,
    all_x, all_g, part_v, x_v, r_v, h_v, gg_v, ug_v, total,
    send_sem, recv_sem, own_sem, out_sem,
):
    me, z, q, qx, qy, qd = place()
    full, own = (all_x, all_g), (x_ref, g_ref)
    cap, ff, chunk = pick.shape[1], gate_w.shape[1], 256
    rows = 4 * cap
    f32, bf16 = jnp.float32, jnp.bfloat16
    greet(me, z, qx, qy)

    def copy_of(zz, a, block, way):
        mine = block is None
        return pltpu.make_async_remote_copy(
            src_ref=own[a] if mine else full[a].at[block],
            dst_ref=full[a].at[me if mine else block],
            send_sem=send_sem.at[a, me if mine else block, way],
            recv_sem=recv_sem.at[a, me if mine else block],
            device_id={"expert": (4 * zz + qx, 4 * zz + qy, me + 4, me - 4)[way]},
        )

    def arrive(a, block):
        pltpu.make_async_remote_copy(
            src_ref=full[a].at[block],
            dst_ref=full[a].at[block],
            send_sem=send_sem.at[a, block, 0],
            recv_sem=recv_sem.at[a, block],
            device_id={"expert": 4 * z + qx},
        ).wait_recv()

    def column_ways(zz, src):
        ways = []
        if src <= zz < DEPTH - 1:
            ways.append(2)
        if src >= zz > 0:
            ways.append(3)
        return ways + [0, 1]

    def column(zz, src):
        for a in range(2):
            if src != zz:
                arrive(a, 4 * src + q)
            for way in column_ways(zz, src):
                copy_of(zz, a, None if src == zz else 4 * src + q, way).start()

    def talk(zz, i):
        order = near_first(zz)
        if i == 0:
            column(zz, zz)
            for a in range(2):
                pltpu.make_async_copy(own[a], full[a].at[me], own_sem.at[a]).start()
        if i + 1 < DEPTH:
            column(zz, order[i + 1])
        if i < DEPTH:
            arrive(1, 4 * order[i] + qx)
            copy_of(zz, 1, 4 * order[i] + qx, 1).start()
            arrive(0, 4 * order[i] + qy)
            copy_of(zz, 0, 4 * order[i] + qy, 0).start()
        if i == 1:
            for a in range(2):
                pltpu.make_async_copy(own[a], full[a].at[me], own_sem.at[a]).wait()
        if i > 0:
            src = order[i - 1]
            arrive(0, 4 * src + qx)
            arrive(1, 4 * src + qy)
            arrive(0, 4 * src + qd)
            arrive(1, 4 * src + qd)

    def finish(zz):
        for src in near_first(zz):
            for a in range(2):
                for way in column_ways(zz, src):
                    copy_of(zz, a, None if src == zz else 4 * src + q, way).wait_send()
            copy_of(zz, 1, 4 * src + qx, 1).wait_send()
            copy_of(zz, 0, 4 * src + qy, 0).wait_send()

    def results(s):
        at = pl.ds(pl.multiple_of(s * rows, rows), rows)
        pairs = [(part_v, part.at[pl.ds(4 * s, 4)]), (x_v, xrows.at[at]), (r_v, row_grad.at[at])]
        pairs += [(h_v, hidden.at[at]), (gg_v, gate_grad.at[at]), (ug_v, up_grad.at[at])]
        return [pltpu.make_async_copy(a, b, out_sem.at[i]) for i, (a, b) in enumerate(pairs)]

    def work(s):
        def compact(p, carry):
            at = pl.ds(pl.multiple_of(p * cap, cap), cap)
            block = 4 * s + p
            x = jnp.dot(pick[block], all_x[block], preferred_element_type=f32)
            x_v[at, :] = x.astype(bf16)
            r = jnp.dot(pick[block], all_g[block], preferred_element_type=f32)
            r_v[at, :] = (r * gates[block]).astype(bf16)
            return carry

        lax.fori_loop(0, 4, compact, 0)
        total[...] = jnp.zeros_like(total)

        def unit(c, carry):
            at = pl.ds(pl.multiple_of(c * chunk, chunk), chunk)
            wg, wu = gate_w[:, at], up_w[:, at]
            pre_gate = jnp.dot(x_v[...], wg, preferred_element_type=f32)
            pre_up = jnp.dot(x_v[...], wu, preferred_element_type=f32)
            hidden_grad = nt(r_v[...], down_w[at, :])
            sig = 1.0 / (1.0 + jnp.exp(-pre_gate))
            act = pre_gate * sig
            h_v[:, at] = (act * pre_up).astype(bf16)
            ug = (hidden_grad * act).astype(bf16)
            gg = (hidden_grad * pre_up * sig * (1.0 + pre_gate * (1.0 - sig))).astype(bf16)
            ug_v[:, at] = ug
            gg_v[:, at] = gg
            total[...] += nt(gg, wg) + nt(ug, wu)
            return carry

        lax.fori_loop(0, ff // chunk, unit, 0)

        def spread(p, carry):
            at = pl.ds(pl.multiple_of(p * cap, cap), cap)
            back = total[at, :].astype(bf16)
            out = jnp.dot(pick_t[4 * s + p], back, preferred_element_type=f32)
            part_v[p] = out.astype(bf16)
            return carry

        lax.fori_loop(0, 4, spread, 0)

    def step(i, carry):
        s = jnp.int32(0)
        for zz in range(DEPTH):
            for j in range(DEPTH + 1):
                here = (z == zz) & (i == j)
                pl.when(here)(lambda zz=zz, j=j: talk(zz, j))
                if j > 0:
                    s = jnp.where(here, near_first(zz)[j - 1], s)

        @pl.when(i > 1)
        def _():
            for copy in results(0):
                copy.wait()

        @pl.when(i > 0)
        def _():
            work(s)
            for copy in results(s):
                copy.start()

        return carry

    lax.fori_loop(0, DEPTH + 1, step, 0)
    for copy in results(0):
        copy.wait()
    for zz in range(DEPTH):
        pl.when(z == zz)(lambda zz=zz: finish(zz))


def routed_rows(inputs, out_grad, pick, pick_t, gates, gate_w, up_w, down_w):
    tokens, width = inputs.shape
    blocks, cap, _ = pick.shape
    ff = gate_w.shape[1]
    dtype = inputs.dtype
    hbm, vmem = pl.BlockSpec(memory_space=pl.ANY), pl.BlockSpec(memory_space=pltpu.VMEM)
    out = [(blocks, tokens, width)] + [(blocks * cap, width)] * 2 + [(blocks * cap, ff)] * 3
    held = [(blocks, tokens, width)] * 2 + [(4, tokens, width)]
    held += [(4 * cap, width)] * 2 + [(4 * cap, ff)] * 3
    return pl.pallas_call(
        rows_kernel,
        out_shape=tuple(jax.ShapeDtypeStruct(shape, dtype) for shape in out),
        in_specs=[vmem] * 8,
        out_specs=(hbm,) * 6,
        scratch_shapes=[pltpu.VMEM(shape, dtype) for shape in held]
        + [
            pltpu.VMEM((4 * cap, width), jnp.float32),
            pltpu.SemaphoreType.DMA((2, 4 * DEPTH, 4)),
            pltpu.SemaphoreType.DMA((2, 4 * DEPTH)),
            pltpu.SemaphoreType.DMA((2,)),
            pltpu.SemaphoreType.DMA((6,)),
        ],
        compiler_params=pltpu.CompilerParams(
            collective_id=0, has_side_effects=True, vmem_limit_bytes=56 * 1024 * 1024
        ),
    )(inputs, out_grad, pick, pick_t, gates, gate_w, up_w, down_w)


def scatter_kernel(
    part, out, halves, far, near, column, above, send_sem, far_sem, near_sem, above_sem
):
    me, z, q, qx, qy, qd = place()
    rows, width = out.shape
    half = width // 2
    cut = (pl.ds(0, half), pl.ds(half, half))
    step = 16
    greet(me, z, qx, qy)

    def total(dst, terms):
        def body(i, carry):
            at = pl.ds(pl.multiple_of(i * step, step), step)
            acc = terms[0][at, :].astype(jnp.float32)
            for term in terms[1:]:
                acc = acc + term[at, :].astype(jnp.float32)
            dst[at, :] = acc.astype(dst.dtype)
            return carry

        lax.fori_loop(0, rows // step, body, 0)

    def at_depth(zz):
        sent = []
        plane = (4 * zz + qx, 4 * zz + qy)

        def send(src_ref, dst_ref, sem, recv, dev):
            copy = pltpu.make_async_remote_copy(
                src_ref=src_ref,
                dst_ref=dst_ref,
                send_sem=sem,
                recv_sem=recv,
                device_id={"expert": dev},
            )
            copy.start()
            sent.append(copy)

        def arrive(ref, recv):
            pltpu.make_async_remote_copy(
                src_ref=ref,
                dst_ref=ref,
                send_sem=send_sem.at[0, 0],
                recv_sem=recv,
                device_id={"expert": plane[0]},
            ).wait_recv()

        def first(s):
            for h in (0, 1):
                send(
                    part.at[4 * s + qd, :, cut[h]],
                    far.at[h, s],
                    send_sem.at[s, h],
                    far_sem.at[h, s],
                    plane[1 - h],
                )
            for way, block in ((0, 4 * s + qx), (1, 4 * s + qy)):
                h = 1 - way
                send(
                    part.at[block, :, cut[h]],
                    near.at[way, h, s],
                    send_sem.at[s, 2 + way],
                    near_sem.at[way, h, s],
                    plane[way],
                )

        def second(s):
            for way, block in ((0, 4 * s + qx), (1, 4 * s + qy)):
                h = way
                arrive(far.at[h, s], far_sem.at[h, s])
                total(halves.at[way, s], [part.at[block, :, cut[h]], far.at[h, s]])
                send(
                    halves.at[way, s],
                    near.at[way, h, s],
                    send_sem.at[s, 4 + way],
                    near_sem.at[way, h, s],
                    plane[way],
                )

        def third(s):
            slots = []
            if s <= zz < DEPTH - 1:
                slots.append(s)
            if s >= zz > 0:
                slots.append(DEPTH if s == zz else s)
            for way in (0, 1):
                for h in (0, 1):
                    arrive(near.at[way, h, s], near_sem.at[way, h, s])
            for slot in slots:
                arrive(above.at[slot], above_sem.at[slot])
            dst = out if s == zz else column.at[s]
            for h in (0, 1):
                terms = [part.at[4 * s + q, :, cut[h]], near.at[0, h, s], near.at[1, h, s]]
                terms += [above.at[slot, :, cut[h]] for slot in slots]
                total(dst.at[:, cut[h]], terms)
            if s != zz:
                nxt = zz - 1 if s < zz else zz + 1
                slot = DEPTH if s > zz and nxt == s else s
                send(
                    column.at[s],
                    above.at[slot],
                    send_sem.at[s, 6],
                    above_sem.at[slot],
                    me - 4 if s < zz else me + 4,
                )

        order = sorted(range(DEPTH), key=lambda s: (-abs(s - zz), s))
        for i in range(DEPTH + 2):
            if i < DEPTH:
                first(order[i])
            if 0 <= i - 1 < DEPTH:
                second(order[i - 1])
            if 0 <= i - 2 < DEPTH:
                third(order[i - 2])
        for copy in sent:
            copy.wait_send()

    for zz in range(DEPTH):
        pl.when(z == zz)(lambda zz=zz: at_depth(zz))


def scatter_sums(part):
    blocks, rows, width = part.shape
    half = width // 2
    dtype = part.dtype
    return pl.pallas_call(
        scatter_kernel,
        out_shape=jax.ShapeDtypeStruct((rows, width), dtype),
        in_specs=[pl.BlockSpec(memory_space=pltpu.VMEM)],
        out_specs=pl.BlockSpec(memory_space=pltpu.VMEM),
        scratch_shapes=[
            pltpu.VMEM((2, DEPTH, rows, half), dtype),
            pltpu.VMEM((2, DEPTH, rows, half), dtype),
            pltpu.VMEM((2, 2, DEPTH, rows, half), dtype),
            pltpu.VMEM((DEPTH, rows, width), dtype),
            pltpu.VMEM((DEPTH + 1, rows, width), dtype),
            pltpu.SemaphoreType.DMA((DEPTH, 7)),
            pltpu.SemaphoreType.DMA((2, DEPTH)),
            pltpu.SemaphoreType.DMA((2, 2, DEPTH)),
            pltpu.SemaphoreType.DMA((DEPTH + 1,)),
        ],
        compiler_params=pltpu.CompilerParams(
            collective_id=1, has_side_effects=True, vmem_limit_bytes=40 * 1024 * 1024
        ),
    )(part)


def dequant(weight, scale):
    rows, cols = weight.shape
    srows, scols = scale.shape
    blocks = weight.reshape(srows, rows // srows, scols, cols // scols).astype(jnp.float32)
    return (blocks * scale[:, None, :, None]).reshape(rows, cols).astype(jnp.bfloat16)


def shards(
    x_quant, x_scale, out_grad, expert_ids, gate_fixed, w_gate, s_gate, w_up, s_up, w_down, s_down
):
    f32, bf16 = jnp.float32, jnp.bfloat16
    tok_rows, width = x_quant.shape
    topk = expert_ids.shape[1]
    experts = lax.axis_size("expert")
    capacity = tok_rows * topk * 5 // (4 * experts)
    blk_width = width // x_scale.shape[1]
    scaled = x_quant.reshape(tok_rows, -1, blk_width).astype(f32) * x_scale[:, :, None]
    inputs = scaled.reshape(tok_rows, width).astype(bf16)
    named = expert_ids[None, :, :] == jnp.arange(experts, dtype=jnp.int32)[:, None, None]
    units = jnp.sum(jnp.where(named, gate_fixed[None], 0), axis=2).astype(f32)
    units = lax.all_to_all(units, "expert", split_axis=0, concat_axis=0, tiled=True)

    chosen = units > 0
    rank = jnp.cumsum(chosen.astype(jnp.int32), axis=1) - 1
    pick = chosen[:, None, :] & (
        rank[:, None, :] == jnp.arange(capacity, dtype=jnp.int32)[None, :, None]
    )
    gates = jnp.sum(jnp.where(pick, units[:, None, :], 0.0), axis=2) / 65536.0
    pick = pick.astype(bf16)

    gate_w = dequant(w_gate[0], s_gate[0])
    up_w = dequant(w_up[0], s_up[0])
    down_w = dequant(w_down[0], s_down[0])
    rows = experts * capacity
    if experts == 4 * DEPTH:
        spread, xrows, row_grad, hidden, gate_grad, up_grad = routed_rows(
            inputs, out_grad, pick, pick.swapaxes(1, 2), gates[:, :, None], gate_w, up_w, down_w
        )
        grad_input = scatter_sums(spread)
    else:
        all_x = lax.all_gather(inputs, "expert", axis=0, tiled=False)
        all_g = lax.all_gather(out_grad, "expert", axis=0, tiled=False)
        xrows = jnp.einsum("ect,etd->ecd", pick, all_x, preferred_element_type=f32)
        xrows = xrows.astype(bf16).reshape(rows, width)
        row_grad = jnp.einsum("ect,etd->ecd", pick, all_g, preferred_element_type=f32)
        row_grad = (row_grad * gates[:, :, None]).astype(bf16).reshape(rows, width)
        pre_gate = jnp.dot(xrows, gate_w, preferred_element_type=f32)
        pre_up = jnp.dot(xrows, up_w, preferred_element_type=f32)
        sig = jax.nn.sigmoid(pre_gate)
        act = pre_gate * sig
        hidden = (act * pre_up).astype(bf16)
        hidden_grad = jnp.dot(row_grad, down_w.T, preferred_element_type=f32)
        up_grad = (hidden_grad * act).astype(bf16)
        gate_grad = (hidden_grad * pre_up * sig * (1.0 + pre_gate * (1.0 - sig))).astype(bf16)
        row_input = jnp.dot(gate_grad, gate_w.T, preferred_element_type=f32)
        row_input = row_input + jnp.dot(up_grad, up_w.T, preferred_element_type=f32)
        back = row_input.astype(bf16).reshape(experts, capacity, width)
        spread = jnp.einsum("ect,ecd->etd", pick, back, preferred_element_type=f32).astype(bf16)
        grad_input = lax.psum_scatter(
            spread.reshape(experts * tok_rows, width), "expert", scatter_dimension=0, tiled=True
        )
    term_gate = jnp.dot(xrows.T, gate_grad, preferred_element_type=f32).astype(bf16)
    term_up = jnp.dot(xrows.T, up_grad, preferred_element_type=f32).astype(bf16)
    term_down = jnp.dot(hidden.T, row_grad, preferred_element_type=f32).astype(bf16)
    sum_gate = lax.psum_scatter(term_gate, "replica", scatter_dimension=1, tiled=True)
    sum_up = lax.psum_scatter(term_up, "replica", scatter_dimension=1, tiled=True)
    sum_down = lax.psum_scatter(term_down, "replica", scatter_dimension=0, tiled=True)
    return (grad_input, sum_gate[None], sum_up[None], sum_down[None])


def solution(mesh):
    tokens = P(("expert", "replica"), None)
    weights = P("expert", None, None)
    return jax.shard_map(
        shards,
        mesh=mesh,
        in_specs=(tokens,) * 5 + (weights,) * 6,
        out_specs=(
            tokens,
            P("expert", None, "replica"),
            P("expert", None, "replica"),
            P("expert", "replica", None),
        ),
        check_vma=False,
    )
```

profile of v0, /device:TPU:14, one launch (start us, length us, event | category | flops | bytes accessed | tf_op | source)
XLA Modules:
  0.0 350.9 jit_solution(1951136815928362746)
XLA Ops:
  7.2 0.7 select_reduce_fusion.1
  7.9 0.6 convert_element_type.68
  8.5 7.1 %all-to-all-start = ((f32[16,1,128]{2,1,0:T(1,128)}), f32[16,1,128]{2,1,0:T(1,128)S(1)}, u32[]{:S(2)}, u32[]{:S(2)}) async-start(f32[16,1,128]{2,1,0:T(1,128)} %bitcast.1), calls=%async_computation | async-start | bytes 16384 | tf_op jit(solution)/shard_map/all_to_all | solution.py:389
  15.6 0.0 reduce-scatter.10.cloned.1.call-start
  15.7 0.7 copy.67
  16.4 0.7 copy.66
  17.1 0.7 copy.65
  17.7 0.8 copy.39
  18.5 0.5 mul.58
  19.0 5.7 %copy.63 = f32[96,8,16,128]{3,1,2,0:T(8,128)} copy(f32[96,8,16,128]{3,2,1,0:T(8,128)S(1)} %bitcast.66) | data formatting | bytes 12582912
  24.7 6.6 %copy.43 = f32[2048,768]{1,0:T(8,128)} copy(f32[2048,768]{0,1:T(8,128)} %bitcast.67) | data formatting | bytes 12582912 | tf_op jit(solution)/shard_map/mul | solution.py:373
  31.3 0.5 mul.54
  31.8 5.6 %copy.64 = f32[96,8,16,128]{3,1,2,0:T(8,128)} copy(f32[96,8,16,128]{3,2,1,0:T(8,128)S(1)} %bitcast.68) | data formatting | bytes 12582912
  37.4 6.5 %copy.42 = f32[2048,768]{1,0:T(8,128)} copy(f32[2048,768]{0,1:T(8,128)} %bitcast.69) | data formatting | bytes 12582912 | tf_op jit(solution)/shard_map/mul | solution.py:373
  44.0 0.0 copy-start.2
  44.0 0.5 mul.62
  44.4 1.4 copy-done.2
  45.9 0.0 copy-start.1
  45.9 4.1 %fusion.down_w = bf16[768,2048]{1,0:T(8,128)(2,1)} fusion(f32[96,8,16,128]{3,2,1,0:T(8,128)S(1)} %bitcast.70, bf16[1,768,2048]{2,1,0:T(8,128)(2,1)S(1)} %copy-done.2), kind=kLoop, calls=%fused_computation.1 | loop fusion | flops 4718592 | bytes 12582912 | tf_op jit(solution)/shard_map/convert_element_type | solution.py:373
  50.0 0.0 copy-done.1
  50.0 9.5 %fusion.1 = (bf16[2048,768]{1,0:T(8,128)(2,1)}, bf16[2048,768]{1,0:T(8,128)(2,1)}) fusion(f32[2048,768]{1,0:T(8,128)} %copy.43, bf16[1,2048,768]{2,1,0:T(8,128)(2,1)S(1)} %copy-done.1, f32[2048,768]{1,0:T(8,128)} %copy.42, bf16[1,2048,768]{2,1,0:T(8,128)(2,1)} %param.16), kind=kLoop, calls=%fused_computation.5 | loop fusion | flops 9437184 | bytes 25165824 | tf_op jit(solution)/shard_map/convert_element_type | solution.py:373
  59.5 0.3 mul.50
  59.8 2.2 fusion.3.x_ref
  62.0 0.0 all-to-all-done
  62.0 0.3 reduce_window_sum.14
  62.3 0.8 fusion.7.pick
  63.1 1.4 fusion.5.pick_t
  64.5 0.4 select_reduce_fusion
  64.9 1.1 copy.44.gates
  66.0 163.9 %shard_map.138 = (bf16[16,128,2048]{2,1,0:T(8,128)(2,1)}, bf16[1280,2048]{1,0:T(8,128)(2,1)}, bf16[1280,2048]{1,0:T(8,128)(2,1)}, bf16[1280,768]{1,0:T(8,128)(2,...) custom-call(bf16[128,2048]{1,0:T(8,128)(2,1)} %fusion.3.x_ref, bf16[128,2048]{1,0:T(8,128)(2,1)} %g_ref.1, ...), custom_call_target="tpu_custom_call" | custom-call | tf_op jit(solution)/shard_map/pallas_call | solution.py:205
  229.9 7.5 %convolution_convert_fusion.2 = bf16[2048,768]{1,0:T(8,128)(2,1)S(1)} fusion(bf16[1280,2048]{1,0:T(8,128)(2,1)} %get-tuple-element.11, bf16[1280,768]{1,0:T(8,128)(2,1)} %get-tuple-element.12), kind=kOutput, calls=%fused_computation.10 | convolution fusion | flops 4028104704 | bytes 10354688 | tf_op jit(solution)/shard_map/dot_general | solution.py:430
  237.4 3.0 copy.45
  240.4 0.0 reduce-scatter.10.cloned.1.call-update
  240.4 0.3 reduce-scatter.12.cloned.1.call-start
  240.7 7.5 %convolution_convert_fusion.1 = bf16[2048,768]{1,0:T(8,128)(2,1)S(1)} fusion(bf16[1280,2048]{1,0:T(8,128)(2,1)} %get-tuple-element.11, bf16[1280,768]{1,0:T(8,128)(2,1)} %get-tuple-element.13), kind=kOutput, calls=%fused_computation.9 | convolution fusion | flops 4028104704 | bytes 10354688 | tf_op jit(solution)/shard_map/dot_general | solution.py:431
  248.2 2.9 copy.47
  251.2 0.0 copy-start.3
  251.2 0.0 reduce-scatter.12.cloned.1.call-update
  251.2 0.0 reduce-scatter.8.cloned.1.call-start
  251.2 1.6 copy-done.3
  252.8 8.2 %convolution_convert_fusion = bf16[768,2048]{1,0:T(8,128)(2,1)} fusion(bf16[1280,768]{1,0:T(8,128)(2,1)S(1)} %copy-done.3, bf16[1280,2048]{1,0:T(8,128)(2,1)} %get-tuple-element.15), kind=kOutput, calls=%fused_computation.8 | convolution fusion | flops 4028104704 | bytes 10354688 | tf_op jit(solution)/shard_map/dot_general | solution.py:432
  261.0 0.0 reduce-scatter.8.cloned.1.call-update
  261.0 0.0 copy-start
  261.0 4.5 %copy-done = bf16[16,128,2048]{2,1,0:T(8,128)(2,1)S(1)} copy-done((bf16[16,128,2048]{2,1,0:T(8,128)(2,1)S(1)}, bf16[16,128,2048]{2,1,0:T(8,128)(2,1)}, u32[]{:S(2)}) %copy-start) | copy-done | bytes 8388632
  265.5 72.9 %shard_map.139 = bf16[128,2048]{1,0:T(8,128)(2,1)S(1)} custom-call(bf16[16,128,2048]{2,1,0:T(8,128)(2,1)S(1)} %copy-done), custom_call_target="tpu_custom_call" | custom-call | tf_op jit(solution)/shard_map/pallas_call | solution.py:347
  338.4 0.0 reduce-scatter.10.cloned.1.call-done
  338.4 2.6 copy.46
  341.0 0.0 reduce-scatter.12.cloned.1.call-done
  341.0 2.6 copy.48
  343.6 0.0 reduce-scatter.8.cloned.1.call-done
  343.6 0.8 copy.69
  (3 shorter events, 0.0 us)
Async XLA Ops:
  8.5 53.5 %all-to-all-start = ((f32[16,1,128]{2,1,0:T(1,128)}), f32[16,1,128]{2,1,0:T(1,128)S(1)}, u32[]{:S(2)}, u32[]{:S(2)}) async-start(f32[16,1,128]{2,1,0:T(1,128)} %bitcast.1), calls=%async_computation | async-start | bytes 16384 | tf_op jit(solution)/shard_map/all_to_all | solution.py:389
  15.6 322.8 %reduce-scatter.10.cloned.1.call-start = ((), (), s32[]{:S(2)}) async-start(), calls=%async_computation.5 | async-start | bytes 4718592
  44.0 1.9 copy-start.2
  45.9 4.1 %copy-start.1 = (bf16[1,2048,768]{2,1,0:T(8,128)(2,1)S(1)}, bf16[1,2048,768]{2,1,0:T(8,128)(2,1)}, u32[]{:S(2)}) copy-start(bf16[1,2048,768]{2,1,0:T(8,128)(2,1)} %param.18) | copy-start | bytes 9437188
  240.4 100.6 %reduce-scatter.12.cloned.1.call-start = ((), (), s32[]{:S(2)}) async-start(), calls=%async_computation.6 | async-start | bytes 4718592
  251.2 1.7 copy-start.3
  251.2 92.4 %reduce-scatter.8.cloned.1.call-start = ((), (), s32[]{:S(2)}) async-start(), calls=%async_computation.4 | async-start | bytes 4718592 | tf_op jit(solution)/shard_map/reduce_scatter | solution.py:435
  261.0 4.5 %copy-start = (bf16[16,128,2048]{2,1,0:T(8,128)(2,1)S(1)}, bf16[16,128,2048]{2,1,0:T(8,128)(2,1)}, u32[]{:S(2)}) copy-start(bf16[16,128,2048]{2,1,0:T(8,128)(2,1)} %get-tuple-element.10.part) | copy-start | bytes 25165828
Sparse Core Ops, SparseCore 0:
  240.5 11.6 reduce-scatter.9
  254.6 12.0 reduce-scatter.11
  269.5 12.0 reduce-scatter.7
where the time goes:
time: 353 us; the launch traced here: 351 us
  Pallas kernels  237 us (67%)
  local copies, waits for them, and re-layouts  49.6 us (14%)
  matrix products  23.1 us (7%)
  other arithmetic  20 us (6%)
  between operations  13.8 us (4%)
  starting transfers between devices  7.52 us (2%)
    pallas_call x1, Pallas kernels, routed_rows(): pl.pallas_call(rows_kernel, out_shape=tuple((jax.ShapeDtypeStruct(shape,...  164 us
    pallas_call x1, Pallas kernels, scatter_sums(): pl.pallas_call(scatter_kernel, out_shape=jax.ShapeDtypeStruct((rows, widt...  72.9 us
    unnamed x19, local copies, waits for them, and re-layouts  33.6 us
    mul x5, local copies, waits for them, and re-layouts, dequant(): blocks * scale[:, None, :, None]  14.5 us
    convert_element_type x2, other arithmetic, dequant(): (blocks * scale[:, None, :, None]).reshape(rows, cols).astype(jnp.bfloat16)  13.6 us
    dot_general x1, matrix products, shards(): jnp.dot(hidden.T, row_grad, preferred_element_type=f32).astype(bf16)  8.15 us
    dot_general x1, matrix products, shards(): term_up = jnp.dot(xrows.T, up_grad, preferred_element_type=f32).astype(bf16)  7.47 us
    dot_general x1, matrix products, shards(): jnp.dot(xrows.T, gate_grad, preferred_element_type=f32).astype(bf16)  7.47 us
  transfers between devices with their start and end apart: 4, of which 0 were waited for; matrix products, arithmetic and copies ran while one was open for 20% of the time, Pallas kernels for 21%

commit v1 on v0

--- a/solution.py
+++ b/solution.py
@@ -15,8 +15,10 @@
     return me, z, q, q + 1 - 2 * x, q + 2 - 4 * y, 3 - q
 
 
-def greet(me, z, qx, qy):
+def greet(me, z, qx, qy, twin=None):
     barrier = pltpu.get_barrier_semaphore()
+    if twin is not None:
+        pl.semaphore_signal(barrier, inc=1, device_id={"replica": twin})
     for dev in (4 * z + qx, 4 * z + qy):
         pl.semaphore_signal(barrier, inc=1, device_id={"expert": dev})
 
@@ -29,7 +31,7 @@
         pl.semaphore_signal(barrier, inc=1, device_id={"expert": me + 4})
 
     peers = 2 + jnp.minimum(z, 1) + jnp.minimum(DEPTH - 1 - z, 1)
-    pl.semaphore_wait(barrier, peers)
+    pl.semaphore_wait(barrier, peers + (twin is not None))
 
 
 def near_first(zz):
@@ -41,14 +43,15 @@
 
 
 def rows_kernel(
-    x_ref, g_ref, pick, pick_t, gates, gate_w, up_w, down_w,
+    x_ref, g_ref, pick, pick_t, gates, gate_q, up_q, down_q, gate_s, up_s, down_s,
     part, xrows, row_grad, hidden, gate_grad, up_grad,
     all_x, all_g, part_v, x_v, r_v, h_v, gg_v, ug_v, total,
-    send_sem, recv_sem, own_sem, out_sem,
+    raw_a, raw_b, raw_c, gate_w, up_w, down_w,
+    send_sem, recv_sem, own_sem, out_sem, raw_sem,
 ):
     me, z, q, qx, qy, qd = place()
     full, own = (all_x, all_g), (x_ref, g_ref)
-    cap, ff, chunk = pick.shape[1], gate_w.shape[1], 256
+    cap, ff, chunk = pick.shape[1], gate_q.shape[1], 256
     rows = 4 * cap
     f32, bf16 = jnp.float32, jnp.bfloat16
     greet(me, z, qx, qy)
@@ -89,10 +92,6 @@
 
     def talk(zz, i):
         order = near_first(zz)
-        if i == 0:
-            column(zz, zz)
-            for a in range(2):
-                pltpu.make_async_copy(own[a], full[a].at[me], own_sem.at[a]).start()
         if i + 1 < DEPTH:
             column(zz, order[i + 1])
         if i < DEPTH:
@@ -164,6 +163,33 @@
 
         lax.fori_loop(0, 4, spread, 0)
 
+    def begin(zz):
+        column(zz, zz)
+        for a in range(2):
+            pltpu.make_async_copy(own[a], full[a].at[me], own_sem.at[a]).start()
+
+    def dequantize(raw, scale, weight):
+        def body(i, carry):
+            at = pl.ds(pl.multiple_of(i * 128, 128), 128)
+            for j in range(weight.shape[1] // 128):
+                cols = pl.ds(j * 128, 128)
+                weight[at, cols] = (raw[at, cols].astype(f32) * scale[i, j]).astype(bf16)
+            return carry
+
+        lax.fori_loop(0, weight.shape[0] // 128, body, 0)
+
+    raws = ((gate_q, raw_a), (up_q, raw_b), (down_q, raw_c))
+    loads = [pltpu.make_async_copy(a, b, raw_sem.at[i]) for i, (a, b) in enumerate(raws)]
+    for zz in range(DEPTH):
+        pl.when(z == zz)(lambda zz=zz: begin(zz))
+    for load in loads:
+        load.start()
+    for load, raw, scale, weight in zip(
+        loads, (raw_a, raw_b, raw_c), (gate_s, up_s, down_s), (gate_w, up_w, down_w)
+    ):
+        load.wait()
+        dequantize(raw, scale, weight)
+
     def step(i, carry):
         s = jnp.int32(0)
         for zz in range(DEPTH):
@@ -193,10 +219,10 @@
         pl.when(z == zz)(lambda zz=zz: finish(zz))
 
 
-def routed_rows(inputs, out_grad, pick, pick_t, gates, gate_w, up_w, down_w):
+def routed_rows(inputs, out_grad, pick, pick_t, gates, weights, scales):
     tokens, width = inputs.shape
     blocks, cap, _ = pick.shape
-    ff = gate_w.shape[1]
+    ff = weights[0].shape[1]
     dtype = inputs.dtype
     hbm, vmem = pl.BlockSpec(memory_space=pl.ANY), pl.BlockSpec(memory_space=pltpu.VMEM)
     out = [(blocks, tokens, width)] + [(blocks * cap, width)] * 2 + [(blocks * cap, ff)] * 3
@@ -205,165 +231,243 @@
     return pl.pallas_call(
         rows_kernel,
         out_shape=tuple(jax.ShapeDtypeStruct(shape, dtype) for shape in out),
-        in_specs=[vmem] * 8,
+        in_specs=[vmem] * 5 + [hbm] * 3 + [pl.BlockSpec(memory_space=pltpu.SMEM)] * 3,
         out_specs=(hbm,) * 6,
         scratch_shapes=[pltpu.VMEM(shape, dtype) for shape in held]
         + [
             pltpu.VMEM((4 * cap, width), jnp.float32),
+            *[pltpu.VMEM(w.shape, dtype) for w in weights * 2],
             pltpu.SemaphoreType.DMA((2, 4 * DEPTH, 4)),
             pltpu.SemaphoreType.DMA((2, 4 * DEPTH)),
             pltpu.SemaphoreType.DMA((2,)),
             pltpu.SemaphoreType.DMA((6,)),
+            pltpu.SemaphoreType.DMA((3,)),
         ],
         compiler_params=pltpu.CompilerParams(
             collective_id=0, has_side_effects=True, vmem_limit_bytes=56 * 1024 * 1024
         ),
-    )(inputs, out_grad, pick, pick_t, gates, gate_w, up_w, down_w)
+    )(inputs, out_grad, pick, pick_t, gates, *weights, *scales)
 
 
 def scatter_kernel(
-    part, out, halves, far, near, column, above, send_sem, far_sem, near_sem, above_sem
+    part, xrows, row_grad, hidden, gate_grad, up_grad,
+    out, sum_gate, sum_up, sum_down,
+    halves, far, near, column, above, give_gate, give_up, give_down, got_gate, got_up, got_down,
+    send_sem, far_sem, near_sem, above_sem, give_sem, got_sem,
 ):
     me, z, q, qx, qy, qd = place()
+    core = lax.axis_index("replica")
     rows, width = out.shape
     half = width // 2
     cut = (pl.ds(0, half), pl.ds(half, half))
     step = 16
-    greet(me, z, qx, qy)
+    f32 = jnp.float32
+    greet(me, z, qx, qy, 1 - core)
 
     def total(dst, terms):
         def body(i, carry):
             at = pl.ds(pl.multiple_of(i * step, step), step)
-            acc = terms[0][at, :].astype(jnp.float32)
+            acc = terms[0][at, :].astype(f32)
             for term in terms[1:]:
-                acc = acc + term[at, :].astype(jnp.float32)
+                acc = acc + term[at, :].astype(f32)
             dst[at, :] = acc.astype(dst.dtype)
             return carry
 
         lax.fori_loop(0, rows // step, body, 0)
 
-    def at_depth(zz):
-        sent = []
+    def copy_of(src_ref, dst_ref, sem, recv, dev):
+        return pltpu.make_async_remote_copy(
+            src_ref=src_ref,
+            dst_ref=dst_ref,
+            send_sem=sem,
+            recv_sem=recv,
+            device_id={"expert": dev},
+        )
+
+    def arrive(ref, recv):
+        copy_of(ref, ref, send_sem.at[0, 0], recv, 4 * z + qx).wait_recv()
+
+    def first(zz, s):
         plane = (4 * zz + qx, 4 * zz + qy)
-
-        def send(src_ref, dst_ref, sem, recv, dev):
-            copy = pltpu.make_async_remote_copy(
-                src_ref=src_ref,
-                dst_ref=dst_ref,
-                send_sem=sem,
-                recv_sem=recv,
-                device_id={"expert": dev},
-            )
-            copy.start()
-            sent.append(copy)
-
-        def arrive(ref, recv):
-            pltpu.make_async_remote_copy(
-                src_ref=ref,
-                dst_ref=ref,
-                send_sem=send_sem.at[0, 0],
-                recv_sem=recv,
-                device_id={"expert": plane[0]},
-            ).wait_recv()
-
-        def first(s):
-            for h in (0, 1):
-                send(
+        copies = []
+        for h in (0, 1):
+            copies.append(
+                copy_of(
                     part.at[4 * s + qd, :, cut[h]],
                     far.at[h, s],
                     send_sem.at[s, h],
                     far_sem.at[h, s],
                     plane[1 - h],
                 )
-            for way, block in ((0, 4 * s + qx), (1, 4 * s + qy)):
-                h = 1 - way
-                send(
+            )
+        for way, block in ((0, 4 * s + qx), (1, 4 * s + qy)):
+            h = 1 - way
+            copies.append(
+                copy_of(
                     part.at[block, :, cut[h]],
                     near.at[way, h, s],
                     send_sem.at[s, 2 + way],
                     near_sem.at[way, h, s],
                     plane[way],
                 )
-
-        def second(s):
-            for way, block in ((0, 4 * s + qx), (1, 4 * s + qy)):
-                h = way
-                arrive(far.at[h, s], far_sem.at[h, s])
-                total(halves.at[way, s], [part.at[block, :, cut[h]], far.at[h, s]])
-                send(
-                    halves.at[way, s],
-                    near.at[way, h, s],
-                    send_sem.at[s, 4 + way],
-                    near_sem.at[way, h, s],
-                    plane[way],
-                )
-
-        def third(s):
-            slots = []
-            if s <= zz < DEPTH - 1:
-                slots.append(s)
-            if s >= zz > 0:
-                slots.append(DEPTH if s == zz else s)
+            )
+        return copies
+
+    def second(zz, s, way):
+        return copy_of(
+            halves.at[way, s],
+            near.at[way, way, s],
+            send_sem.at[s, 4 + way],
+            near_sem.at[way, way, s],
+            4 * zz + (qx, qy)[way],
+        )
+
+    def third(zz, s):
+        slot = DEPTH if s > zz and zz + 1 == s else s
+        return copy_of(
+            column.at[s],
+            above.at[slot],
+            send_sem.at[s, 6],
+            above_sem.at[slot],
+            me - 4 if s < zz else me + 4,
+        )
+
+    def relay(zz, s):
+        for way, block in ((0, 4 * s + qx), (1, 4 * s + qy)):
+            arrive(far.at[way, s], far_sem.at[way, s])
+            total(halves.at[way, s], [part.at[block, :, cut[way]], far.at[way, s]])
+            second(zz, s, way).start()
+
+    def add(zz, s):
+        slots = []
+        if s <= zz < DEPTH - 1:
+            slots.append(s)
+        if s >= zz > 0:
+            slots.append(DEPTH if s == zz else s)
+        for way in (0, 1):
+            for h in (0, 1):
+                arrive(near.at[way, h, s], near_sem.at[way, h, s])
+        for slot in slots:
+            arrive(above.at[slot], above_sem.at[slot])
+        dst = out if s == zz else column.at[s]
+        for h in (0, 1):
+            terms = [part.at[4 * s + q, :, cut[h]], near.at[0, h, s], near.at[1, h, s]]
+            terms += [above.at[slot, :, cut[h]] for slot in slots]
+            total(dst.at[:, cut[h]], terms)
+        if s != zz:
+            third(zz, s).start()
+
+    def talk(zz, i):
+        order = near_first(zz)[::-1]
+        if i < DEPTH:
+            for copy in first(zz, order[i]):
+                copy.start()
+        if 0 <= i - 1 < DEPTH:
+            relay(zz, order[i - 1])
+        if 0 <= i - 2 < DEPTH:
+            add(zz, order[i - 2])
+
+    def finish(zz):
+        for s in range(DEPTH):
+            for copy in first(zz, s):
+                copy.wait_send()
             for way in (0, 1):
-                for h in (0, 1):
-                    arrive(near.at[way, h, s], near_sem.at[way, h, s])
-            for slot in slots:
-                arrive(above.at[slot], above_sem.at[slot])
-            dst = out if s == zz else column.at[s]
-            for h in (0, 1):
-                terms = [part.at[4 * s + q, :, cut[h]], near.at[0, h, s], near.at[1, h, s]]
-                terms += [above.at[slot, :, cut[h]] for slot in slots]
-                total(dst.at[:, cut[h]], terms)
+                second(zz, s, way).wait_send()
             if s != zz:
-                nxt = zz - 1 if s < zz else zz + 1
-                slot = DEPTH if s > zz and nxt == s else s
-                send(
-                    column.at[s],
-                    above.at[slot],
-                    send_sem.at[s, 6],
-                    above_sem.at[slot],
-                    me - 4 if s < zz else me + 4,
-                )
-
-        order = sorted(range(DEPTH), key=lambda s: (-abs(s - zz), s))
-        for i in range(DEPTH + 2):
-            if i < DEPTH:
-                first(order[i])
-            if 0 <= i - 1 < DEPTH:
-                second(order[i - 1])
-            if 0 <= i - 2 < DEPTH:
-                third(order[i - 2])
-        for copy in sent:
-            copy.wait_send()
-
+                third(zz, s).wait_send()
+
+    lots = (
+        (xrows, gate_grad, give_gate, got_gate, sum_gate),
+        (xrows, up_grad, give_up, got_up, sum_up),
+        (hidden, row_grad, give_down, got_down, sum_down),
+    )
+
+    def give(k):
+        return pltpu.make_async_remote_copy(
+            src_ref=lots[k][2],
+            dst_ref=lots[k][3],
+            send_sem=give_sem.at[k],
+            recv_sem=got_sem.at[k],
+            device_id={"replica": 1 - core},
+        )
+
+    def product(k, side, emit):
+        left, right = lots[k][:2]
+        chunk = 512
+        ff = hidden.shape[1] // 2
+        units = pl.ds(pl.multiple_of(side * ff, ff), ff)
+
+        def body(c, carry):
+            at = pl.ds(pl.multiple_of(c * chunk, chunk), chunk)
+            a = left[:, at] if k < 2 else left[:, units]
+            b = right[:, units] if k < 2 else right[:, at]
+            acc = lax.dot_general(a, b, (((0,), (0,)), ((), ())), preferred_element_type=f32)
+            emit((at, slice(None)) if k < 2 else (slice(None), at), acc)
+            return carry
+
+        lax.fori_loop(0, width // chunk, body, 0)
+
+    def work(k, last):
+        kept, got, dst = lots[k][2:]
+
+        def emit_other(at, acc):
+            kept[at] = acc.astype(kept.dtype)
+
+        def emit_own(at, acc):
+            dst[at] = (acc + got[at].astype(f32)).astype(dst.dtype)
+
+        if last:
+            give(k).wait_recv()
+            product(k, core, emit_own)
+        else:
+            product(k, 1 - core, emit_other)
+            give(k).start()
+
+    def turn(i, carry):
+        for j in range(DEPTH + 2):
+            for zz in range(DEPTH):
+                pl.when((z == zz) & (i == j))(lambda zz=zz, j=j: talk(zz, j))
+            pl.when(i == j)(lambda j=j: work(j % 3, j >= 3))
+        return carry
+
+    lax.fori_loop(0, DEPTH + 2, turn, 0)
+    for k in range(3):
+        give(k).wait_send()
     for zz in range(DEPTH):
-        pl.when(z == zz)(lambda zz=zz: at_depth(zz))
-
-
-def scatter_sums(part):
+        pl.when(z == zz)(lambda zz=zz: finish(zz))
+
+
+def scatter_sums(part, xrows, row_grad, hidden, gate_grad, up_grad):
     blocks, rows, width = part.shape
-    half = width // 2
+    half, ff = width // 2, hidden.shape[1] // 2
     dtype = part.dtype
+    vmem = pl.BlockSpec(memory_space=pltpu.VMEM)
+    lots = [(width, ff), (width, ff), (ff, width)]
+    held = [
+        (2, DEPTH, rows, half),
+        (2, DEPTH, rows, half),
+        (2, 2, DEPTH, rows, half),
+        (DEPTH, rows, width),
+        (DEPTH + 1, rows, width),
+    ]
     return pl.pallas_call(
         scatter_kernel,
-        out_shape=jax.ShapeDtypeStruct((rows, width), dtype),
-        in_specs=[pl.BlockSpec(memory_space=pltpu.VMEM)],
-        out_specs=pl.BlockSpec(memory_space=pltpu.VMEM),
-        scratch_shapes=[
-            pltpu.VMEM((2, DEPTH, rows, half), dtype),
-            pltpu.VMEM((2, DEPTH, rows, half), dtype),
-            pltpu.VMEM((2, 2, DEPTH, rows, half), dtype),
-            pltpu.VMEM((DEPTH, rows, width), dtype),
-            pltpu.VMEM((DEPTH + 1, rows, width), dtype),
+        out_shape=tuple(jax.ShapeDtypeStruct(shape, dtype) for shape in [(rows, width), *lots]),
+        in_specs=[vmem] * 6,
+        out_specs=(vmem,) * 4,
+        scratch_shapes=[pltpu.VMEM(shape, dtype) for shape in held + lots + lots]
+        + [
             pltpu.SemaphoreType.DMA((DEPTH, 7)),
             pltpu.SemaphoreType.DMA((2, DEPTH)),
             pltpu.SemaphoreType.DMA((2, 2, DEPTH)),
             pltpu.SemaphoreType.DMA((DEPTH + 1,)),
+            pltpu.SemaphoreType.DMA((3,)),
+            pltpu.SemaphoreType.DMA((3,)),
         ],
         compiler_params=pltpu.CompilerParams(
-            collective_id=1, has_side_effects=True, vmem_limit_bytes=40 * 1024 * 1024
+            collective_id=1, has_side_effects=True, vmem_limit_bytes=58 * 1024 * 1024
         ),
-    )(part)
+    )(part, xrows, row_grad, hidden, gate_grad, up_grad)
 
 
 def dequant(weight, scale):
@@ -396,37 +500,44 @@
     gates = jnp.sum(jnp.where(pick, units[:, None, :], 0.0), axis=2) / 65536.0
     pick = pick.astype(bf16)
 
+    if experts == 4 * DEPTH:
+        moved = routed_rows(
+            inputs,
+            out_grad,
+            pick,
+            pick.swapaxes(1, 2),
+            gates[:, :, None],
+            [w_gate[0], w_up[0], w_down[0]],
+            [s_gate[0], s_up[0], s_down[0]],
+        )
+        grad_input, sum_gate, sum_up, sum_down = scatter_sums(*moved)
+        return (grad_input, sum_gate[None], sum_up[None], sum_down[None])
+
     gate_w = dequant(w_gate[0], s_gate[0])
     up_w = dequant(w_up[0], s_up[0])
     down_w = dequant(w_down[0], s_down[0])
     rows = experts * capacity
-    if experts == 4 * DEPTH:
-        spread, xrows, row_grad, hidden, gate_grad, up_grad = routed_rows(
-            inputs, out_grad, pick, pick.swapaxes(1, 2), gates[:, :, None], gate_w, up_w, down_w
-        )
-        grad_input = scatter_sums(spread)
-    else:
-        all_x = lax.all_gather(inputs, "expert", axis=0, tiled=False)
-        all_g = lax.all_gather(out_grad, "expert", axis=0, tiled=False)
-        xrows = jnp.einsum("ect,etd->ecd", pick, all_x, preferred_element_type=f32)
-        xrows = xrows.astype(bf16).reshape(rows, width)
-        row_grad = jnp.einsum("ect,etd->ecd", pick, all_g, preferred_element_type=f32)
-        row_grad = (row_grad * gates[:, :, None]).astype(bf16).reshape(rows, width)
-        pre_gate = jnp.dot(xrows, gate_w, preferred_element_type=f32)
-        pre_up = jnp.dot(xrows, up_w, preferred_element_type=f32)
-        sig = jax.nn.sigmoid(pre_gate)
-        act = pre_gate * sig
-        hidden = (act * pre_up).astype(bf16)
-        hidden_grad = jnp.dot(row_grad, down_w.T, preferred_element_type=f32)
-        up_grad = (hidden_grad * act).astype(bf16)
-        gate_grad = (hidden_grad * pre_up * sig * (1.0 + pre_gate * (1.0 - sig))).astype(bf16)
-        row_input = jnp.dot(gate_grad, gate_w.T, preferred_element_type=f32)
-        row_input = row_input + jnp.dot(up_grad, up_w.T, preferred_element_type=f32)
-        back = row_input.astype(bf16).reshape(experts, capacity, width)
-        spread = jnp.einsum("ect,ecd->etd", pick, back, preferred_element_type=f32).astype(bf16)
-        grad_input = lax.psum_scatter(
-            spread.reshape(experts * tok_rows, width), "expert", scatter_dimension=0, tiled=True
-        )
+    all_x = lax.all_gather(inputs, "expert", axis=0, tiled=False)
+    all_g = lax.all_gather(out_grad, "expert", axis=0, tiled=False)
+    xrows = jnp.einsum("ect,etd->ecd", pick, all_x, preferred_element_type=f32)
+    xrows = xrows.astype(bf16).reshape(rows, width)
+    row_grad = jnp.einsum("ect,etd->ecd", pick, all_g, preferred_element_type=f32)
+    row_grad = (row_grad * gates[:, :, None]).astype(bf16).reshape(rows, width)
+    pre_gate = jnp.dot(xrows, gate_w, preferred_element_type=f32)
+    pre_up = jnp.dot(xrows, up_w, preferred_element_type=f32)
+    sig = jax.nn.sigmoid(pre_gate)
+    act = pre_gate * sig
+    hidden = (act * pre_up).astype(bf16)
+    hidden_grad = jnp.dot(row_grad, down_w.T, preferred_element_type=f32)
+    up_grad = (hidden_grad * act).astype(bf16)
+    gate_grad = (hidden_grad * pre_up * sig * (1.0 + pre_gate * (1.0 - sig))).astype(bf16)
+    row_input = jnp.dot(gate_grad, gate_w.T, preferred_element_type=f32)
+    row_input = row_input + jnp.dot(up_grad, up_w.T, preferred_element_type=f32)
+    back = row_input.astype(bf16).reshape(experts, capacity, width)
+    spread = jnp.einsum("ect,ecd->etd", pick, back, preferred_element_type=f32).astype(bf16)
+    grad_input = lax.psum_scatter(
+        spread.reshape(experts * tok_rows, width), "expert", scatter_dimension=0, tiled=True
+    )
     term_gate = jnp.dot(xrows.T, gate_grad, preferred_element_type=f32).astype(bf16)
     term_up = jnp.dot(xrows.T, up_grad, preferred_element_type=f32).astype(bf16)
     term_down = jnp.dot(hidden.T, row_grad, preferred_element_type=f32).astype(bf16)

time: 353 us -> 281 us (0.80)
  local copies, waits for them, and re-layouts: 49.6 us -> 12 us
  matrix products: 23.1 us -> 0 us
  Pallas kernels: 237 us -> 252 us
  other arithmetic: 20 us -> 6.42 us
  between operations: 13.8 us -> 0.71 us
    unnamed x19 -> x16, local copies, waits for them, and re-layouts: 33.6 us -> 9.23 us
    dot_general x3 -> x0, matrix products: 23.1 us -> none  [the longest x1 8.15 us: shards(): jnp.dot(hidden.T, row_grad, preferred_element_type=f32).astype(bf16)]
    pallas_call x1, Pallas kernels: 72.9 us -> 91 us  [scatter_sums(): pl.pallas_call(scatter_kernel, out_shape=tuple((jax.ShapeDtypeStruct(shap...]
    mul x5 -> x0, local copies, waits for them, and re-layouts: 14.5 us -> none  [dequant(): blocks * scale[:, None, :, None]]
    convert_element_type x2 -> x0, other arithmetic: 13.6 us -> none  [dequant(): (blocks * scale[:, None, :, None]).reshape(rows, cols).astype(jnp.bfloat16)]
  transfers between devices with their start and end apart: 4 -> 1, of which waited for: 0 -> 0; matrix products, arithmetic and copies ran while one was open for 20% -> 2% of each run, Pallas kernels for 21% -> 0%
where the time goes in v1:
time: 281 us; the launch traced here: 278 us
  Pallas kernels  252 us (90%)
  local copies, waits for them, and re-layouts  12 us (4%)
  starting transfers between devices  7.14 us (3%)
  other arithmetic  6.42 us (2%)
    pallas_call x1, Pallas kernels, routed_rows(): pl.pallas_call(rows_kernel, out_shape=tuple((jax.ShapeDtypeStruct(shape,...  161 us
    pallas_call x1, Pallas kernels, scatter_sums(): pl.pallas_call(scatter_kernel, out_shape=tuple((jax.ShapeDtypeStruct(shap...  91 us
    unnamed x16, local copies, waits for them, and re-layouts  9.23 us
    all_to_all x1, starting transfers between devices, shards(): lax.all_to_all(units, 'expert', split_axis=0, concat_axis=0, tiled=True)  7.14 us
  transfers between devices with their start and end apart: 1, of which 0 were waited for; matrix products, arithmetic and copies ran while one was open for 2% of the time, Pallas kernels for 0%

profile of v1, /device:TPU:14, one launch (start us, length us, event | category | flops | bytes accessed | tf_op | source)
XLA Modules:
  0.0 278.2 jit_solution(12957205718235044906)
XLA Ops:
  0.6 0.0 copy-start.2
  0.6 0.0 copy-start.3
  0.7 0.0 copy-start.4
  0.7 0.7 select_reduce_fusion.1
  1.4 0.6 convert_element_type.29
  2.0 7.1 %all-to-all-start = ((f32[16,1,128]{2,1,0:T(1,128)}), f32[16,1,128]{2,1,0:T(1,128)S(1)}, u32[]{:S(2)}, u32[]{:S(2)}) async-start(f32[16,1,128]{2,1,0:T(1,128)} %bitcast.1), calls=%async_computation | async-start | bytes 16384 | tf_op jit(solution)/shard_map/all_to_all | solution.py:493
  9.2 0.8 copy.39
  9.9 0.3 mul.11
  10.3 2.2 fusion.x_ref
  12.5 0.0 copy-done.2
  12.5 0.6 copy.51
  13.1 0.0 copy-done.3
  13.1 0.7 copy.45
  13.7 0.0 copy-done.4
  13.7 0.7 copy.46
  14.4 0.0 all-to-all-done
  14.4 0.3 reduce_window_sum.14
  14.7 0.8 fusion.4.pick
  15.6 1.4 fusion.2.pick_t
  17.0 0.4 select_reduce_fusion
  17.3 1.1 copy.42.gates
  18.5 160.9 %shard_map.138 = (bf16[16,128,2048]{2,1,0:T(8,128)(2,1)}, bf16[1280,2048]{1,0:T(8,128)(2,1)}, bf16[1280,2048]{1,0:T(8,128)(2,1)}, bf16[1280,768]{1,0:T(8,128)(2,...) custom-call(bf16[128,2048]{1,0:T(8,128)(2,1)} %fusion.x_ref, bf16[128,2048]{1,0:T(8,128)(2,1)} %g_ref.1, ...), custom_call_target="tpu_custom_call" | custom-call | tf_op jit(solution)/shard_map/pallas_call | solution.py:231
  179.3 91.0 %shard_map.139 = (bf16[128,2048]{1,0:T(8,128)(2,1)}, bf16[2048,384]{1,0:T(8,128)(2,1)}, bf16[2048,384]{1,0:T(8,128)(2,1)}, bf16[384,2048]{1,0:T(8,128)(2,1)}) custom-call(bf16[16,128,2048]{2,1,0:T(8,128)(2,1)} %get-tuple-element.14.part, bf16[1280,2048]{1,0:T(8,128)(2,1)} %get-tuple-element.15.xrows, bf16[1280,2048]{1,0:T(8,128)(2,1)} %get-tuple-element.16.row_grad, ...), custom_call_target="tpu_custom_call" | custom-call | tf_op jit(solution)/shard_map/pallas_call | solution.py:453
  270.3 0.0 copy-start.1
  270.3 2.0 copy.56
  272.3 2.7 copy.57
  275.0 0.0 copy-done.1
  275.0 0.0 copy-start
  275.0 1.1 copy.58
  276.2 0.8 copy-done
  277.0 1.1 copy.59
  (3 shorter events, 0.0 us)
Async XLA Ops:
  0.6 11.8 %copy-start.2 = (f32[1,6,16]{2,0,1:T(1,128)S(1)}, f32[1,6,16]{2,0,1:T(1,128)}, u32[]{:S(2)}) copy-start(f32[1,6,16]{2,0,1:T(1,128)} %param.21) | copy-start | bytes 1156
  0.6 12.4 %copy-start.3 = (f32[1,16,6]{1,0,2:T(1,128)S(1)}, f32[1,16,6]{1,0,2:T(1,128)}, u32[]{:S(2)}) copy-start(f32[1,16,6]{1,0,2:T(1,128)} %param.17) | copy-start | bytes 1156
  0.7 13.1 %copy-start.4 = (f32[1,16,6]{1,0,2:T(1,128)S(1)}, f32[1,16,6]{1,0,2:T(1,128)}, u32[]{:S(2)}) copy-start(f32[1,16,6]{1,0,2:T(1,128)} %param.19) | copy-start | bytes 1156
  2.0 12.4 %all-to-all-start = ((f32[16,1,128]{2,1,0:T(1,128)}), f32[16,1,128]{2,1,0:T(1,128)S(1)}, u32[]{:S(2)}, u32[]{:S(2)}) async-start(f32[16,1,128]{2,1,0:T(1,128)} %bitcast.1), calls=%async_computation | async-start | bytes 16384 | tf_op jit(solution)/shard_map/all_to_all | solution.py:493
  270.3 4.7 %copy-start.1 = (bf16[2048,384]{1,0:T(8,128)(2,1)S(1)}, bf16[2048,384]{1,0:T(8,128)(2,1)}, u32[]{:S(2)}) copy-start(bf16[2048,384]{1,0:T(8,128)(2,1)} %get-tuple-element.22) | copy-start | bytes 4718596
  275.0 2.0 copy-start

commit v2 on v1

--- a/solution.py
+++ b/solution.py
@@ -359,8 +359,8 @@
 
     def talk(zz, i):
         order = near_first(zz)[::-1]
-        if i < DEPTH:
-            for copy in first(zz, order[i]):
+        for s in order[:2] if i == 0 else order[i + 1 : i + 2]:
+            for copy in first(zz, s):
                 copy.start()
         if 0 <= i - 1 < DEPTH:
             relay(zz, order[i - 1])
@@ -425,9 +425,12 @@
 
     def turn(i, carry):
         for j in range(DEPTH + 2):
+            if j == DEPTH + 1:
+                pl.when(i == j)(lambda j=j: work(j % 3, j >= 3))
             for zz in range(DEPTH):
                 pl.when((z == zz) & (i == j))(lambda zz=zz, j=j: talk(zz, j))
-            pl.when(i == j)(lambda j=j: work(j % 3, j >= 3))
+            if j < DEPTH + 1:
+                pl.when(i == j)(lambda j=j: work(j % 3, j >= 3))
         return carry
 
     lax.fori_loop(0, DEPTH + 2, turn, 0)

time: 281 us -> 289 us (1.028)
  Pallas kernels: 252 us -> 258 us
    pallas_call x1, Pallas kernels: 91 us -> 97.4 us  [scatter_sums(): pl.pallas_call(scatter_kernel, out_shape=tuple((jax.ShapeDtypeStruct(shap...]
where the time goes in v2:
time: 289 us; the launch traced here: 285 us
  Pallas kernels  258 us (89%)
  local copies, waits for them, and re-layouts  12 us (4%)
  starting transfers between devices  7.14 us (2%)
  other arithmetic  6.42 us (2%)
    pallas_call x1, Pallas kernels, routed_rows(): pl.pallas_call(rows_kernel, out_shape=tuple((jax.ShapeDtypeStruct(shape,...  161 us
    pallas_call x1, Pallas kernels, scatter_sums(): pl.pallas_call(scatter_kernel, out_shape=tuple((jax.ShapeDtypeStruct(shap...  97.4 us
    unnamed x16, local copies, waits for them, and re-layouts  9.23 us
    all_to_all x1, starting transfers between devices, shards(): lax.all_to_all(units, 'expert', split_axis=0, concat_axis=0, tiled=True)  7.14 us
  transfers between devices with their start and end apart: 1, of which 0 were waited for; matrix products, arithmetic and copies ran while one was open for 2% of the time, Pallas kernels for 0%

profile of v2, /device:TPU:14, one launch (start us, length us, event | category | flops | bytes accessed | tf_op | source)
XLA Modules:
  0.0 284.6 jit_solution(17901204134427073592)
XLA Ops:
  0.6 0.0 copy-start.2
  0.6 0.0 copy-start.3
  0.7 0.0 copy-start.4
  0.7 0.7 select_reduce_fusion.1
  1.4 0.6 convert_element_type.29
  2.0 7.1 %all-to-all-start = ((f32[16,1,128]{2,1,0:T(1,128)}), f32[16,1,128]{2,1,0:T(1,128)S(1)}, u32[]{:S(2)}, u32[]{:S(2)}) async-start(f32[16,1,128]{2,1,0:T(1,128)} %bitcast.1), calls=%async_computation | async-start | bytes 16384 | tf_op jit(solution)/shard_map/all_to_all | solution.py:496
  9.2 0.8 copy.39
  9.9 0.3 mul.11
  10.3 2.2 fusion.x_ref
  12.5 0.0 copy-done.2
  12.5 0.6 copy.51
  13.1 0.0 copy-done.3
  13.1 0.7 copy.45
  13.7 0.0 copy-done.4
  13.7 0.7 copy.46
  14.4 0.0 all-to-all-done
  14.4 0.3 reduce_window_sum.14
  14.7 0.8 fusion.4.pick
  15.6 1.4 fusion.2.pick_t
  17.0 0.4 select_reduce_fusion
  17.3 1.1 copy.42.gates
  18.5 160.9 %shard_map.138 = (bf16[16,128,2048]{2,1,0:T(8,128)(2,1)}, bf16[1280,2048]{1,0:T(8,128)(2,1)}, bf16[1280,2048]{1,0:T(8,128)(2,1)}, bf16[1280,768]{1,0:T(8,128)(2,...) custom-call(bf16[128,2048]{1,0:T(8,128)(2,1)} %fusion.x_ref, bf16[128,2048]{1,0:T(8,128)(2,1)} %g_ref.1, ...), custom_call_target="tpu_custom_call" | custom-call | tf_op jit(solution)/shard_map/pallas_call | solution.py:231
  179.3 97.4 %shard_map.139 = (bf16[128,2048]{1,0:T(8,128)(2,1)}, bf16[2048,384]{1,0:T(8,128)(2,1)}, bf16[2048,384]{1,0:T(8,128)(2,1)}, bf16[384,2048]{1,0:T(8,128)(2,1)}) custom-call(bf16[16,128,2048]{2,1,0:T(8,128)(2,1)} %get-tuple-element.14.part, bf16[1280,2048]{1,0:T(8,128)(2,1)} %get-tuple-element.15.xrows, bf16[1280,2048]{1,0:T(8,128)(2,1)} %get-tuple-element.16.row_grad, ...), custom_call_target="tpu_custom_call" | custom-call | tf_op jit(solution)/shard_map/pallas_call | solution.py:456
  276.7 0.0 copy-start.1
  276.7 2.0 copy.56
  278.7 2.7 copy.57
  281.5 0.0 copy-done.1
  281.5 0.0 copy-start
  281.5 1.1 copy.58
  282.6 0.8 copy-done
  283.4 1.1 copy.59
  (3 shorter events, 0.0 us)
Async XLA Ops:
  0.6 11.8 %copy-start.2 = (f32[1,6,16]{2,0,1:T(1,128)S(1)}, f32[1,6,16]{2,0,1:T(1,128)}, u32[]{:S(2)}) copy-start(f32[1,6,16]{2,0,1:T(1,128)} %param.21) | copy-start | bytes 1156
  0.6 12.4 %copy-start.3 = (f32[1,16,6]{1,0,2:T(1,128)S(1)}, f32[1,16,6]{1,0,2:T(1,128)}, u32[]{:S(2)}) copy-start(f32[1,16,6]{1,0,2:T(1,128)} %param.17) | copy-start | bytes 1156
  0.7 13.1 %copy-start.4 = (f32[1,16,6]{1,0,2:T(1,128)S(1)}, f32[1,16,6]{1,0,2:T(1,128)}, u32[]{:S(2)}) copy-start(f32[1,16,6]{1,0,2:T(1,128)} %param.19) | copy-start | bytes 1156
  2.0 12.4 %all-to-all-start = ((f32[16,1,128]{2,1,0:T(1,128)}), f32[16,1,128]{2,1,0:T(1,128)S(1)}, u32[]{:S(2)}, u32[]{:S(2)}) async-start(f32[16,1,128]{2,1,0:T(1,128)} %bitcast.1), calls=%async_computation | async-start | bytes 16384 | tf_op jit(solution)/shard_map/all_to_all | solution.py:496
  276.7 4.7 %copy-start.1 = (bf16[2048,384]{1,0:T(8,128)(2,1)S(1)}, bf16[2048,384]{1,0:T(8,128)(2,1)}, u32[]{:S(2)}) copy-start(bf16[2048,384]{1,0:T(8,128)(2,1)} %get-tuple-element.22) | copy-start | bytes 4718596
  281.5 2.0 copy-start
